TPU v7x, 512 devices: a whole 4x4x16 slice. The times are simulated.
512 devices in a mesh: row: 16 (over x, z_lo), col: 32 (over z_hi, y, core).
Axes of the slice: x: 4, y: 4, z: 16 (z_hi: 4, z_lo: 4; z = z_hi * 4 + z_lo), core: 2. Of those that a mesh axis runs over, the one named last changes fastest.
Arguments:
- spectra: bfloat16 [2048, 2, 128, 128], P(('row', 'col')), may hold values from -3600 to 3600
- kept_windows: int32 [128], replicated, may hold values 0 or 1
Outputs:
- correlations: float32 [2048, 32, 64, 128], P('row', 'col')
All inputs are finite; a program needn't handle non-finite values.
Results may differ from a plain program's by a relative error of at most 0.0025.
Values may be sent and summed in bfloat16 or wider, within the bound.
A program may use at most 128 MiB of HBM per device.

v0:
```python
import math

import jax
import jax.numpy as jnp
from jax import lax
from jax.sharding import PartitionSpec as P

EPSILON = 1e-06


def make_lag_table(bins_count, windows):
    bin_ids = jnp.arange(bins_count, dtype=jnp.int32)
    phase_index = bin_ids[:, None] * bin_ids[None, :] % bins_count
    phases = phase_index.astype(jnp.float32) * (2.0 * math.pi / bins_count)
    norming = 1.0 / math.sqrt(bins_count * windows)
    return jnp.stack([jnp.cos(phases) * norming, -jnp.sin(phases) * norming], axis=1)


def partner_operand(col_rows):
    real_part = col_rows[:, 0]
    imag_part = col_rows[:, 1]
    re_half = jnp.concatenate([real_part, imag_part], axis=2)
    im_half = jnp.concatenate([-imag_part, real_part], axis=2)
    return jnp.concatenate([re_half, im_half], axis=0)


def cross_lags(first_rows, partner, lag_table):
    first_half = jnp.concatenate([first_rows[:, 0], first_rows[:, 1]], axis=2)
    stacks = lax.dot_general(
        first_half, partner, (((2,), (2,)), ((1,), (1,))), preferred_element_type=jnp.float32
    )
    partners_count = partner.shape[0] // 2
    stacks = stacks.reshape(stacks.shape[0], stacks.shape[1], 2, partners_count)
    return jnp.einsum("fmps,fpk->msk", stacks, lag_table, precision=lax.Precision.HIGHEST)


def body(spectra, kept_windows):
    bins_count = spectra.shape[2]
    windows = spectra.shape[3]
    own_float = spectra.astype(jnp.float32)
    partial_energy = jnp.sum(own_float * own_float, axis=(0, 1, 2))
    channels = spectra.shape[0] * lax.axis_size("row") * lax.axis_size("col")
    energy_sum = lax.psum(partial_energy, ("row", "col"))
    energy = energy_sum / (channels * 2 * bins_count) + EPSILON
    factor = kept_windows.astype(jnp.float32) / energy
    column_block = lax.all_gather(spectra, "row", axis=0, tiled=True)
    partner = partner_operand(column_block)
    lag_table = make_lag_table(bins_count, windows)
    row_block = lax.all_gather(spectra, "col", axis=0, tiled=True)
    lag_rows = cross_lags(
        (row_block.astype(jnp.float32) * factor).astype(jnp.bfloat16), partner, lag_table
    )
    return lag_rows[:, None]


def solution(mesh):
    placed = (P(("row", "col"), None, None, None), P())
    return jax.shard_map(
        body, mesh=mesh, in_specs=placed, out_specs=P("row", "col", None, None), check_vma=False
    )
```

profile of v0, /device:TPU:6, one launch (start us, length us, event | category | flops | bytes accessed | tf_op | source)
XLA Modules:
  0.0 313.1 jit_solution(12809178669511933960)
XLA Ops:
  6.5 0.0 all-gather.5.cloned.1.call-start
  6.5 0.7 all-gather.5.cloned.1.call-update
  7.3 0.0 all-gather.3.cloned.1.call-start
  7.3 0.7 all-gather.3.cloned.1.call-update
  8.0 1.1 multiply_reduce_fusion
  9.1 110.6 %psum.7 = f32[128]{0:T(128)S(1)} all-reduce(f32[128]{0:T(128)S(1)} %multiply_reduce_fusion), channel_id=1, replica_groups=mesh['row'=16,'col'=32] {'row','col'}, use_global_device_ids=true, to_apply=%region_1.0 | all-reduce | flops 128 | bytes 1024 | tf_op jit(solution)/shard_map/psum | solution.py:43
  119.7 0.3 negate_multiply_fusion
  120.0 0.7 add_divide_fusion
  120.7 0.9 all-gather.5.cloned.1.call-done
  121.6 2.7 fusion.27
  124.3 2.9 fusion.26
  127.2 4.6 %copy_bitcast_fusion = (bf16[64,128,128]{2,0,1:T(8,128)(2,1)}, bf16[64,128,128]{2,0,1:T(8,128)(2,1)}) fusion(bf16[64,1,128,128]{3,2,1,0:T(8,128)(2,1)S(1)} %get-tuple-element.7, bf16[64,1,128,128]{3,2,1,0:T(8,128)(2,1)S(1)} %get-tuple-element.8), kind=kLoop, calls=%fused_computation.17 | loop fusion | bytes 8388608 | tf_op jit(solution)/shard_map/squeeze | solution.py:21
  131.9 127.8 %all-gather.3.cloned.1.call-done = bf16[128,2,128,128]{3,2,1,0:T(8,128)(2,1)} async-done(((bf16[4,2,128,128]{3,2,1,0:T(8,128)(2,1)}), bf16[128,2,128,128]{3,2,1,0:T(8,128)(2,1)}) %all-gather.3.cloned.1.call-update) | async-done | bytes 8388624 | tf_op jit(solution)/shard_map/all_gather | solution.py:49
  259.6 12.0 %multiply_convert_fusion = bf16[128,2,128,128]{3,0,2,1:T(8,128)(2,1)} fusion(bf16[128,2,128,128]{3,2,1,0:T(8,128)(2,1)} %all-gather.3.cloned.1.call-done, f32[128]{0:T(128)S(1)} %add_divide_fusion), kind=kLoop, calls=%fused_computation | loop fusion | flops 12582912 | bytes 16777728 | tf_op jit(solution)/shard_map/convert_element_type | solution.py:51
  271.6 6.1 %slice_bitcast_fusion.1 = (bf16[128,128,128]{2,0,1:T(8,128)(2,1)}, bf16[128,128,128]{2,0,1:T(8,128)(2,1)}) fusion(bf16[128,2,128,128]{3,0,2,1:T(8,128)(2,1)} %multiply_convert_fusion), kind=kLoop, calls=%fused_computation.15 | loop fusion | bytes 16777216 | tf_op jit(solution)/shard_map/squeeze | solution.py:28
  277.8 7.1 %fusion = f32[128,128,128]{1,2,0:T(8,128)S(1)} fusion(bf16[128,128,128]{2,0,1:T(8,128)(2,1)} %get-tuple-element.6, bf16[128,128,128]{2,0,1:T(8,128)(2,1)} %get-tuple-element.5, bf16[64,128,128]{2,0,1:T(8,128)(2,1)} %get-tuple-element.10, bf16[64,128,128]{2,0,1:T(8,128)(2,1)} %fusion.26, bf16[64,128,128]{2,0,1:T(8,128)(2,1)} %get-tuple-element.9), kind=kOutput, calls=%fused_computation.1 | convolution fusion | flops 1124073472 | bytes 23068672 | tf_op jit(solution)/shard_map/dot_general | solution.py:29
  284.9 16.9 %fusion.13 = f32[128,1,64,128]{3,0,2,1:T(8,128)S(1)} fusion(f32[128,128,2,64]{1,3,2,0:T(8,128)S(1)} %bitcast.18, f32[128,1,128]{2,0,1:T(8,128)S(1)} %get-tuple-element.11, f32[128,1,128]{2,0,1:T(8,128)S(1)} %get-tuple-element.12), kind=kOutput, calls=%fused_computation.16 | convolution fusion | flops 3221258240 | bytes 12713984 | tf_op jit(solution)/shard_map/fmps,fpk->msk/dot_general | solution.py:34
  301.8 4.4 %copy.11 = f32[128,1,64,128]{3,2,1,0:T(8,128)} copy(f32[128,1,64,128]{3,0,2,1:T(8,128)S(1)} %fusion.13) | data formatting | bytes 8388608 | tf_op jit(solution)/shard_map/broadcast_in_dim | solution.py:53
Async XLA Ops:
  6.5 115.0 %all-gather.5.cloned.1.call-start = ((), (), s32[]{:S(2)}) async-start(), calls=%async_computation.1 | async-start | bytes 4456448 | tf_op jit(solution)/shard_map/all_gather | solution.py:46
  7.3 252.4 %all-gather.3.cloned.1.call-start = ((), (), s32[]{:S(2)}) async-start(), calls=%async_computation | async-start | bytes 8650752 | tf_op jit(solution)/shard_map/all_gather | solution.py:49
Sparse Core Ops, SparseCore 0:
  9.4 112.0 all-gather.4
  124.7 134.8 all-gather.2
where the time goes:
time: 314 us; the launch traced here: 313 us
  waiting for transfers between devices  130 us (41%)
  blocking collectives  111 us (35%)
  matrix products  24 us (8%)
  local copies, waits for them, and re-layouts  17.9 us (6%)
  other arithmetic  17 us (5%)
  between operations  13.4 us (4%)
    all_gather x1, waiting for transfers between devices, body(): row_block = lax.all_gather(spectra, 'col', axis=0, tiled=True)  128 us
    psum x1, blocking collectives, body(): energy_sum = lax.psum(partial_energy, ('row', 'col'))  111 us
    dot_general x1, matrix products, cross_lags(): jnp.einsum('fmps,fpk->msk', stacks, lag_table, precision=lax.Precision.HI...  16.9 us
    convert_element_type x1, other arithmetic, body(): (row_block.astype(jnp.float32) * factor).astype(jnp.bfloat16)  12 us
    dot_general x1, matrix products, cross_lags(): lax.dot_general(first_half, partner, (((2,), (2,)), ((1,), (1,))), prefer...  7.12 us
  transfers between devices with their start and end apart: 2, of which 2 were waited for; matrix products, arithmetic and copies ran while one was open for 4% of the time, Pallas kernels for 0%

commit v1 on v0

v1 whole, which is shorter than its diff:
```python
import functools
import math

import jax
import jax.numpy as jnp
import numpy as np
from jax import lax
from jax.experimental import pallas as pl
from jax.experimental.pallas import tpu as pltpu
from jax.sharding import PartitionSpec as P

EPSILON = 1e-06
MESH = pl.DeviceIdType.MESH
WAVES = 2
CHUNK = 16
WAVE = 2 * CHUNK
REACH = ((8, 4), (4, 8))
ORDER = [(0, 1), (1, 0)]
for _s in range(2, 9):
    ORDER += [(0, _s), (1, _s - 1)]
ORDER += [(1, 8)]


def gather_stack(spectra, kept, stack, zbuf, abuf, bbuf, tmp, ebuf, factor,
                 zs, zr, xs, xr, xs2, xr2, ys, yr, ys2, yr2, cs, cr, la, lb, es, er):
    row = lax.axis_index("row")
    col = lax.axis_index("col")
    x, zl = row // 4, row % 4
    zh, y, core = col // 8, (col // 2) % 4, col % 2
    z = zh * 4 + zl

    def at(dx=0, dy=0, dz=0, dzl=0, dzh=0, dc=0):
        new_z = (z + dz + 16) % 16
        new_zl = (new_z % 4 + dzl) % 4
        new_zh = (new_z // 4 + dzh) % 4
        return (
            (x + dx + 4) % 4 * 4 + new_zl,
            new_zh * 8 + (y + dy + 4) % 4 * 2 + (core + dc) % 2,
        )

    peers = [at(dz=1), at(dz=-1), at(dc=1)]
    for p in (1, 2, 3):
        peers += [at(dx=p), at(dy=p), at(dzl=p), at(dzh=p)]
    barrier = pltpu.get_barrier_semaphore()
    for peer in peers:
        pl.semaphore_signal(barrier, inc=1, device_id=peer, device_id_type=MESH)

    channels = spectra.shape[0]
    total = jnp.zeros((8, 128), jnp.float32)
    for part in range(2):
        for t in range(channels):
            plane = spectra[t, part].astype(jnp.float32)
            total = total + jnp.sum((plane * plane).reshape(16, 8, 128), axis=0)
            tmp[pl.ds(part * channels + t, 128, stride=8), :] = plane
    zbuf[z] = tmp[...].reshape(64, 16, 128).astype(jnp.bfloat16)
    pl.semaphore_wait(barrier, len(peers))

    def remote(src, dst, send, recv, device):
        return pltpu.make_async_remote_copy(
            src_ref=src, dst_ref=dst, send_sem=send, recv_sem=recv, device_id=device, device_id_type=MESH
        )

    rounds = [("dx", x, 4), ("dy", y, 4), ("dzl", zl, 4), ("dzh", zh, 4), ("dc", core, 2)]

    def energy_copies(k):
        name, place, size = rounds[k]
        return [
            remote(ebuf.at[k, place], ebuf.at[k, place], es.at[k, p], er.at[k, p], at(**{name: p}))
            for p in range(1, size)
        ]

    def energy_start(k, value):
        ebuf[k, rounds[k][1]] = value
        for copy in energy_copies(k):
            copy.start()

    def energy_finish(k):
        for copy in energy_copies(k):
            copy.wait()
        return jnp.sum(ebuf[k, : rounds[k][2]], axis=0)

    def z_copy(side, s, w, h):
        slot = (z - s + 16) % 16 if side == 0 else (z + s) % 16
        part = zbuf.at[slot, pl.ds(w * WAVE + h * CHUNK, CHUNK)]
        return remote(part, part, zs.at[side, s, w, h], zr.at[side, s, w, h], at(dz=1 if side == 0 else -1))

    def z_arrived(side, s, w, h):
        slot = (z - s + 16) % 16 if side == 0 else (z + s) % 16
        part = zbuf.at[slot, pl.ds(w * WAVE + h * CHUNK, CHUNK)]
        remote(part, part, zs.at[side, s - 1, w, h], zr.at[side, s - 1, w, h], at(dz=1)).wait_recv()

    def wave(w):
        return pl.ds(w * WAVE, WAVE)

    def half(w, h):
        return pl.ds(w * WAVE + h * CHUNK, CHUNK)

    def x_first(side, unit, w):
        return remote(
            zbuf.at[zh * 4 + unit, wave(w)], bbuf.at[x * 4 + unit, wave(w)],
            xs.at[side, unit, w], xr.at[side, unit, w], at(dx=1 if side == 0 else -1),
        )

    def x_source(side, unit):
        return (x + (3 if side == 0 else 1)) % 4 * 4 + unit

    def x_arrived(side, unit, w):
        part = bbuf.at[x_source(side, unit), wave(w)]
        remote(part, part, xs.at[side, unit, w], xr.at[side, unit, w], at(dx=1)).wait_recv()

    def x_second(side, unit, w):
        part = bbuf.at[x_source(side, unit), half(w, side)]
        return remote(part, part, xs2.at[side, unit, w], xr2.at[side, unit, w], at(dx=1 if side == 0 else -1))

    def x_second_arrived(side, unit, w):
        part = bbuf.at[(x + 2) % 4 * 4 + unit, half(w, side)]
        remote(part, part, xs2.at[side, unit, w], xr2.at[side, unit, w], at(dx=1)).wait_recv()

    def z_high(unit):
        return (zh + (0, 3, 1, 2)[unit]) % 4

    def y_first(side, unit, w):
        return remote(
            zbuf.at[z_high(unit) * 4 + zl, wave(w)], abuf.at[z_high(unit) * 4 + y, core, wave(w)],
            ys.at[side, unit, w], yr.at[side, unit, w], at(dy=1 if side == 0 else -1),
        )

    def y_slot(unit, dy):
        return z_high(unit) * 4 + (y + dy + 4) % 4

    def y_arrived(side, unit, w):
        part = abuf.at[y_slot(unit, -1 if side == 0 else 1), core, wave(w)]
        remote(part, part, ys.at[side, unit, w], yr.at[side, unit, w], at(dy=1)).wait_recv()

    def y_second(side, unit, w):
        part = abuf.at[y_slot(unit, -1 if side == 0 else 1), core, half(w, side)]
        return remote(part, part, ys2.at[side, unit, w], yr2.at[side, unit, w], at(dy=1 if side == 0 else -1))

    def y_second_arrived(side, unit, w):
        part = abuf.at[y_slot(unit, 2), core, half(w, side)]
        remote(part, part, ys2.at[side, unit, w], yr2.at[side, unit, w], at(dy=1)).wait_recv()

    def core_copy(which, unit, w):
        slot = y_slot(unit, (0, -1, 1, 2)[which])
        src = zbuf.at[z_high(unit) * 4 + zl, wave(w)] if which == 0 else abuf.at[slot, core, wave(w)]
        return remote(src, abuf.at[slot, core, wave(w)], cs.at[which, unit, w], cr.at[which, unit, w], at(dc=1))

    def core_arrived(which, unit, w):
        slot = y_slot(unit, (0, -1, 1, 2)[which])
        part = abuf.at[slot, 1 - core, wave(w)]
        remote(part, part, cs.at[which, unit, w], cr.at[which, unit, w], at(dc=1)).wait_recv()

    def own_a(unit, w):
        return pltpu.make_async_copy(
            zbuf.at[z_high(unit) * 4 + zl, wave(w)], abuf.at[y_slot(unit, 0), core, wave(w)], la.at[unit, w]
        )

    def own_b(w):
        return pltpu.make_async_copy(
            zbuf.at[pl.ds(zh * 4, 4), wave(w)], bbuf.at[pl.ds(x * 4, 4), wave(w)], lb.at[w]
        )

    def y_send(unit, w):
        y_first(0, unit, w).start()
        y_first(1, unit, w).start()
        core_copy(0, unit, w).start()
        own_a(unit, w).start()

    def y_pass(unit, w):
        for side in range(2):
            y_arrived(side, unit, w)
            y_second(side, unit, w).start()
            core_copy(1 + side, unit, w).start()

    def y_end(unit, w):
        y_second_arrived(0, unit, w)
        y_second_arrived(1, unit, w)
        core_copy(3, unit, w).start()

    def x_send(unit, w):
        x_first(0, unit, w).start()
        x_first(1, unit, w).start()

    def x_pass(unit, w):
        for side in range(2):
            x_arrived(side, unit, w)
            x_second(side, unit, w).start()

    def in_block(s, act):
        if s == 0:
            act(zl)
        elif s < 4:
            pl.when(zl >= s)(lambda: act(zl - s))
            pl.when(zl + s < 4)(lambda: act(zl + s))

    def z_step(w, s):
        if s == 0:
            for side in range(2):
                for h in ((0, 1) if side == 0 else (1, 0)):
                    z_copy(side, 0, w, h).start()
        else:
            for h in range(2):
                for side in ((0, 1) if h == 0 else (1, 0)):
                    if s <= REACH[h][side]:
                        z_arrived(side, s, w, h)
                        if s < REACH[h][side]:
                            z_copy(side, s, w, h).start()
        if s == 0:
            y_send(0, w)
        if s == 4:
            y_send(1, w)
            y_send(2, w)
        if s == 8:
            y_send(3, w)
        in_block(s, lambda unit: x_send(unit, w))
        if s == 3:
            own_b(w).start()
        if s >= 2:
            in_block(s - 2, lambda unit: x_pass(unit, w))
        if s == 2:
            y_pass(0, w)
        if s == 4:
            y_end(0, w)
        if s == 6:
            y_pass(1, w)
            y_pass(2, w)
        if s == 8:
            y_end(1, w)
            y_end(2, w)

    energy_start(0, total)
    z_step(0, 0)
    stage = 0
    for w, s in ORDER:
        z_step(w, s)
        if w == 0 and stage < 5:
            value = energy_finish(stage)
            stage += 1
            if stage < 5:
                energy_start(stage, value)
            else:
                members = channels * lax.axis_size("row") * lax.axis_size("col")
                energy = jnp.sum(value, axis=0, keepdims=True) / (members * 2 * 128) + EPSILON
                factor[...] = kept[...].astype(jnp.float32) / energy

    def finish(w):
        y_pass(3, w)
        y_end(3, w)
        for unit in range(4):
            for side in range(2):
                x_second_arrived(side, unit, w)
        own_b(w).wait()
        for unit in range(4):
            own_a(unit, w).wait()
        for which in range(4):
            for unit in range(4):
                core_arrived(which, unit, w)

    low_rows = lax.broadcasted_iota(jnp.int32, (1, 8, 128), 1) < 4

    def split_parts(both):
        even, odd = both[:, 0], both[:, 1]
        real = jnp.where(low_rows, even, pltpu.roll(odd, 4, 1))
        imag = jnp.where(low_rows, pltpu.roll(even, 4, 1), odd)
        return real, imag

    def stack_pair(pair, carry):
        first = abuf[:, :, pair].astype(jnp.float32)
        second = bbuf[:, pair].astype(jnp.float32).reshape(8, 2, 16, 128)
        weight = factor[...].reshape(1, 1, 128)
        for odd in range(2):
            real, imag = split_parts(first[:, :, odd * 8 : odd * 8 + 8])
            left = jnp.concatenate(
                [(real * weight).reshape(128, 128), (imag * weight).reshape(128, 128)], axis=1
            ).astype(jnp.bfloat16)
            real, imag = split_parts(second[:, :, odd * 8 : odd * 8 + 8])
            real, imag = real.reshape(64, 128), imag.reshape(64, 128)
            right = jnp.concatenate(
                [jnp.concatenate([real, imag], axis=1), jnp.concatenate([-imag, real], axis=1)], axis=0
            ).astype(jnp.bfloat16)
            stack[2 * pair + odd] = lax.dot_general(
                left, right, (((1,), (1,)), ((), ())), preferred_element_type=jnp.float32
            )
        return carry

    for w in range(WAVES):
        finish(w)
        lax.fori_loop(w * WAVE, (w + 1) * WAVE, stack_pair, 0)

    for w in range(WAVES):
        for side in range(2):
            for h in range(2):
                for s in range(REACH[h][side]):
                    z_copy(side, s, w, h).wait_send()
            for unit in range(4):
                x_first(side, unit, w).wait_send()
                x_second(side, unit, w).wait_send()
                y_first(side, unit, w).wait_send()
                y_second(side, unit, w).wait_send()
        for which in range(4):
            for unit in range(4):
                core_copy(which, unit, w).wait_send()


A_BLK = 8


def lag_kernel(stack, high, low, out):
    first = pl.program_id(0) * A_BLK
    rows = []
    for i in range(A_BLK):
        bins = stack[:, pl.ds(first + i, 1), :].reshape(128, 128).astype(jnp.bfloat16)
        flipped = bins.T
        rows.append(jnp.concatenate([flipped[:64], flipped[64:]], axis=1))
    left = jnp.concatenate(rows, axis=0)
    lags = jnp.dot(left, high[...], preferred_element_type=jnp.float32)
    lags = lags + jnp.dot(left, low[...], preferred_element_type=jnp.float32)
    out[...] = lags.reshape(A_BLK, 1, 64, 128)


def lag_tables():
    bins = np.arange(128)
    phases = (bins[:, None] * bins[None, :] % 128) * (2.0 * math.pi / 128)
    table = np.concatenate([np.cos(phases), -np.sin(phases)], axis=0) / math.sqrt(128 * 128)
    high = table.astype(jnp.bfloat16)
    low = (table - high.astype(np.float64)).astype(jnp.bfloat16)
    return high, low


def body(spectra, kept_windows):
    dma = pltpu.SemaphoreType.DMA
    vmem = pl.BlockSpec(memory_space=pltpu.VMEM)
    stack = pl.pallas_call(
        gather_stack,
        out_shape=jax.ShapeDtypeStruct((128, 128, 128), jnp.float32),
        in_specs=[vmem, vmem],
        out_specs=vmem,
        scratch_shapes=[
            pltpu.VMEM((16, 64, 16, 128), jnp.bfloat16),
            pltpu.VMEM((16, 2, 64, 16, 128), jnp.bfloat16),
            pltpu.VMEM((16, 64, 16, 128), jnp.bfloat16),
            pltpu.VMEM((1024, 128), jnp.float32),
            pltpu.VMEM((5, 4, 8, 128), jnp.float32),
            pltpu.VMEM((1, 128), jnp.float32),
            dma((2, 8, 2, 2)), dma((2, 8, 2, 2)),
            dma((2, 4, 2)), dma((2, 4, 2)), dma((2, 4, 2)), dma((2, 4, 2)),
            dma((2, 4, 2)), dma((2, 4, 2)), dma((2, 4, 2)), dma((2, 4, 2)),
            dma((4, 4, 2)), dma((4, 4, 2)),
            dma((4, 2)), dma((2,)),
            dma((5, 4)), dma((5, 4)),
        ],
        compiler_params=pltpu.CompilerParams(
            collective_id=0, has_side_effects=True, vmem_limit_bytes=40 << 20
        ),
        name="gather_stack",
    )(spectra, kept_windows.reshape(1, 128))
    high, low = lag_tables()
    return pl.pallas_call(
        lag_kernel,
        grid=(128 // A_BLK,),
        out_shape=jax.ShapeDtypeStruct((128, 1, 64, 128), jnp.float32),
        in_specs=[vmem, vmem, vmem],
        out_specs=pl.BlockSpec((A_BLK, 1, 64, 128), lambda i: (i, 0, 0, 0)),
        compiler_params=pltpu.CompilerParams(vmem_limit_bytes=40 << 20),
        name="lags",
    )(stack, jnp.asarray(high), jnp.asarray(low))


def solution(mesh):
    placed = (P(("row", "col"), None, None, None), P())
    return jax.shard_map(
        body, mesh=mesh, in_specs=placed, out_specs=P("row", "col", None, None), check_vma=False
    )
```

time: 314 us -> 103 us (0.33)
  waiting for transfers between devices: 130 us -> 0 us
  blocking collectives: 111 us -> 0 us
  Pallas kernels: 0 us -> 99.3 us
  matrix products: 24 us -> 0 us
  other arithmetic: 17 us -> 0 us
  local copies, waits for them, and re-layouts: 17.9 us -> 1.61 us
  between operations: 13.4 us -> 0.03 us
    all_gather x2 -> x0, waiting for transfers between devices: 129 us -> none  [the longest x1 128 us: body(): row_block = lax.all_gather(spectra, 'col', axis=0, tiled=True)]
    psum x1 -> x0, blocking collectives: 111 us -> none  [body(): energy_sum = lax.psum(partial_energy, ('row', 'col'))]
    pallas_call x0 -> x2, Pallas kernels: none -> 99.3 us  [the longest x1 86.5 us: body(): pl.pallas_call(gather_stack, out_shape=jax.ShapeDtypeStruct((128, 128, 12...]
    dot_general x2 -> x0, matrix products: 24 us -> none  [the longest x1 16.9 us: cross_lags(): jnp.einsum('fmps,fpk->msk', stacks, lag_table, precision=lax.Precision.HI...]
    convert_element_type x1 -> x0, other arithmetic: 12 us -> none  [body(): (row_block.astype(jnp.float32) * factor).astype(jnp.bfloat16)]
    squeeze x2 -> x0, local copies, waits for them, and re-layouts: 10.8 us -> none  [the longest x1 6.13 us: cross_lags(): first_half = jnp.concatenate([first_rows[:, 0], first_rows[:, 1]], axis=2)]
    broadcast_in_dim x1 -> x0, local copies, waits for them, and re-layouts: 4.44 us -> none  [body(): return lag_rows[:, None]]
  transfers between devices with their start and end apart: 2 -> 0, of which waited for: 2 -> 0; matrix products, arithmetic and copies ran while one was open for 4% -> 0% of each run, Pallas kernels for 0% -> 0%
where the time goes in v1:
time: 103 us; the launch traced here: 101 us
  Pallas kernels  99.3 us (96%)
  local copies, waits for them, and re-layouts  1.61 us (2%)
    pallas_call x1, Pallas kernels, body(): pl.pallas_call(gather_stack, out_shape=jax.ShapeDtypeStruct((128, 128, 12...  86.5 us
    pallas_call x1, Pallas kernels, body(): pl.pallas_call(lag_kernel, grid=(128 // A_BLK,), out_shape=jax.ShapeDtype...  12.8 us

profile of v1, /device:TPU:6, one launch (start us, length us, event | category | flops | bytes accessed | tf_op | source)
XLA Modules:
  0.0 100.9 jit_solution(3320801402763790496)
XLA Ops:
  0.0 0.0 copy-start
  0.0 0.9 copy-done
  1.0 0.0 copy-start.3
  1.0 0.7 copy-done.3
  1.6 0.0 copy-start.1
  1.6 0.0 copy-start.2
  1.6 86.5 %gather_stack.1.stack = f32[128,128,128]{2,1,0:T(8,128)S(1)} custom-call(bf16[4,2,128,128]{3,2,1,0:T(8,128)(2,1)S(1)} %copy-done, s32[1,128]{1,0:T(1,128)S(1)} %bitcast.1), custom_call_target="tpu_custom_call" | custom-call | tf_op jit(solution)/shard_map/gather_stack/pallas_call | solution.py:333
  88.1 0.0 copy-done.1
  88.1 0.0 copy-done.2
  88.1 12.8 %lags.1 = f32[128,1,64,128]{3,2,1,0:T(8,128)} custom-call(f32[128,128,128]{2,1,0:T(8,128)S(1)} %gather_stack.1.stack, bf16[256,128]{1,0:T(8,128)(2,1)S(1)} %copy-done.2, bf16[256,128]{1,0:T(8,128)(2,1)S(1)} %copy-done.1), custom_call_target="tpu_custom_call" | custom-call | tf_op jit(solution)/shard_map/lags/pallas_call | solution.py:358
Async XLA Ops:
  0.0 0.9 copy-start
  1.0 0.7 copy-start.3
  1.6 86.5 %copy-start.1 = (bf16[256,128]{1,0:T(8,128)(2,1)S(1)}, bf16[256,128]{1,0:T(8,128)(2,1)}, u32[]{:S(2)}) copy-start(bf16[256,128]{1,0:T(8,128)(2,1)} %constant.5.clone.low) | copy-start | bytes 196612
  1.6 86.5 %copy-start.2 = (bf16[256,128]{1,0:T(8,128)(2,1)S(1)}, bf16[256,128]{1,0:T(8,128)(2,1)}, u32[]{:S(2)}) copy-start(bf16[256,128]{1,0:T(8,128)(2,1)} %constant.4.clone.high) | copy-start | bytes 196612

commit v2 on v1

--- a/solution.py
+++ b/solution.py
@@ -15,14 +15,13 @@
 CHUNK = 16
 WAVE = 2 * CHUNK
 REACH = ((8, 4), (4, 8))
-ORDER = [(0, 1), (1, 0)]
-for _s in range(2, 9):
-    ORDER += [(0, _s), (1, _s - 1)]
-ORDER += [(1, 8)]
-
-
-def gather_stack(spectra, kept, stack, zbuf, abuf, bbuf, tmp, ebuf, factor,
-                 zs, zr, xs, xr, xs2, xr2, ys, yr, ys2, yr2, cs, cr, la, lb, es, er):
+ORDER = [(1, 0)] + [(_w, _s) for _s in range(1, 9) for _w in range(WAVES)]
+TILES = 64
+STEP = 8
+
+
+def gather_stack(spectra_hbm, kept_hbm, stack, zbuf, abuf, bbuf, rhs, spectra, kept, tmp, ebuf, factor,
+                 zs, zr, xs, xr, xs2, xr2, ys, yr, ys2, yr2, cs, cr, la, lb, es, er, ls):
     row = lax.axis_index("row")
     col = lax.axis_index("col")
     x, zl = row // 4, row % 4
@@ -45,14 +44,25 @@
     for peer in peers:
         pl.semaphore_signal(barrier, inc=1, device_id=peer, device_id_type=MESH)
 
+    loads = [pltpu.make_async_copy(spectra_hbm, spectra, ls.at[0]), pltpu.make_async_copy(kept_hbm, kept, ls.at[1])]
+    for load in loads:
+        load.start()
+    for load in loads:
+        load.wait()
+
     channels = spectra.shape[0]
+    to = lax.broadcasted_iota(jnp.int32, (TILES, TILES), 0)
+    source = lax.broadcasted_iota(jnp.int32, (TILES, TILES), 1)
+    mirror = ((to + source == TILES) | (to + source == 0)).astype(jnp.float32).astype(jnp.bfloat16)
     total = jnp.zeros((8, 128), jnp.float32)
     for part in range(2):
         for t in range(channels):
             plane = spectra[t, part].astype(jnp.float32)
             total = total + jnp.sum((plane * plane).reshape(16, 8, 128), axis=0)
-            tmp[pl.ds(part * channels + t, 128, stride=8), :] = plane
-    zbuf[z] = tmp[...].reshape(64, 16, 128).astype(jnp.bfloat16)
+            mirrored = jnp.dot(mirror, spectra[t, part, TILES:], preferred_element_type=jnp.float32)
+            tmp[pl.ds(part * channels + t, TILES, stride=16), :] = plane[:TILES]
+            tmp[pl.ds(8 + part * channels + t, TILES, stride=16), :] = mirrored
+    zbuf[z] = tmp[...].reshape(TILES, 16, 128).astype(jnp.bfloat16)
     pl.semaphore_wait(barrier, len(peers))
 
     def remote(src, dst, send, recv, device):
@@ -243,18 +253,16 @@
                 energy = jnp.sum(value, axis=0, keepdims=True) / (members * 2 * 128) + EPSILON
                 factor[...] = kept[...].astype(jnp.float32) / energy
 
-    def finish(w):
-        y_pass(3, w)
-        y_end(3, w)
+    def finish_b(w):
         for unit in range(4):
             for side in range(2):
                 x_second_arrived(side, unit, w)
         own_b(w).wait()
-        for unit in range(4):
-            own_a(unit, w).wait()
+
+    def finish_a(unit, w):
+        own_a(unit, w).wait()
         for which in range(4):
-            for unit in range(4):
-                core_arrived(which, unit, w)
+            core_arrived(which, unit, w)
 
     low_rows = lax.broadcasted_iota(jnp.int32, (1, 8, 128), 1) < 4
 
@@ -262,30 +270,59 @@
         even, odd = both[:, 0], both[:, 1]
         real = jnp.where(low_rows, even, pltpu.roll(odd, 4, 1))
         imag = jnp.where(low_rows, pltpu.roll(even, 4, 1), odd)
-        return real, imag
-
-    def stack_pair(pair, carry):
-        first = abuf[:, :, pair].astype(jnp.float32)
-        second = bbuf[:, pair].astype(jnp.float32).reshape(8, 2, 16, 128)
-        weight = factor[...].reshape(1, 1, 128)
-        for odd in range(2):
-            real, imag = split_parts(first[:, :, odd * 8 : odd * 8 + 8])
-            left = jnp.concatenate(
-                [(real * weight).reshape(128, 128), (imag * weight).reshape(128, 128)], axis=1
-            ).astype(jnp.bfloat16)
-            real, imag = split_parts(second[:, :, odd * 8 : odd * 8 + 8])
-            real, imag = real.reshape(64, 128), imag.reshape(64, 128)
-            right = jnp.concatenate(
-                [jnp.concatenate([real, imag], axis=1), jnp.concatenate([-imag, real], axis=1)], axis=0
-            ).astype(jnp.bfloat16)
-            stack[2 * pair + odd] = lax.dot_general(
-                left, right, (((1,), (1,)), ((), ())), preferred_element_type=jnp.float32
+        return real.reshape(-1, 128), imag.reshape(-1, 128)
+
+    def over_tiles(w, act):
+        def step(i, carry):
+            for k in range(STEP):
+                act(w * WAVE + i * STEP + k)
+            return carry
+
+        lax.fori_loop(0, WAVE // STEP, step, 0)
+
+    def make_rhs(tile):
+        second = bbuf[:, tile].astype(jnp.float32).reshape(8, 2, 16, 128)
+        real, imag = split_parts(second[:, :, :8])
+        real_m, imag_m = split_parts(second[:, :, 8:])
+        ends = tile == 0
+        keep = jnp.where(ends, 0.0, 1.0)
+        upper = jnp.concatenate([real, imag, real_m * keep, imag_m * keep], axis=1)
+        lower = jnp.concatenate(
+            [-imag * keep, real * keep, jnp.where(ends, real_m, imag_m), jnp.where(ends, imag_m, -real_m)], axis=1
+        )
+        rhs[tile] = jnp.concatenate([upper, lower], axis=0).astype(jnp.bfloat16)
+
+    def make_stack(units):
+        def act(tile):
+            weight = factor[...]
+            rows = []
+            for unit in units:
+                first = abuf[pl.ds(z_high(unit) * 4, 4), :, tile].astype(jnp.float32)
+                parts = split_parts(first[:, :, :8]) + split_parts(first[:, :, 8:])
+                rows.append(jnp.concatenate([part * weight for part in parts], axis=1).astype(jnp.bfloat16))
+            sums = lax.dot_general(
+                jnp.concatenate(rows, axis=0), rhs[tile], (((1,), (1,)), ((), ())), preferred_element_type=jnp.float32
             )
-        return carry
+            for i, unit in enumerate(units):
+                stack[pl.ds(z_high(unit) * (32 * TILES) + tile, 32, stride=TILES), :] = sums[32 * i : 32 * i + 32]
+
+        return act
 
     for w in range(WAVES):
-        finish(w)
-        lax.fori_loop(w * WAVE, (w + 1) * WAVE, stack_pair, 0)
+        finish_b(w)
+        over_tiles(w, make_rhs)
+        y_pass(3, w)
+    for w in range(WAVES):
+        finish_a(0, w)
+        over_tiles(w, make_stack([0]))
+    for w in range(WAVES):
+        y_end(3, w)
+        finish_a(1, w)
+        finish_a(2, w)
+        over_tiles(w, make_stack([1, 2]))
+    for w in range(WAVES):
+        finish_a(3, w)
+        over_tiles(w, make_stack([3]))
 
     for w in range(WAVES):
         for side in range(2):
@@ -302,26 +339,35 @@
                 core_copy(which, unit, w).wait_send()
 
 
-A_BLK = 8
+A_BLK = 32
 
 
 def lag_kernel(stack, high, low, out):
     first = pl.program_id(0) * A_BLK
     rows = []
-    for i in range(A_BLK):
-        bins = stack[:, pl.ds(first + i, 1), :].reshape(128, 128).astype(jnp.bfloat16)
-        flipped = bins.T
+    for i in range(0, A_BLK, 2):
+        start = pl.multiple_of((first + i) * TILES, 2 * TILES)
+        flipped = stack[pl.ds(start, 2 * TILES), :].astype(jnp.bfloat16).T
         rows.append(jnp.concatenate([flipped[:64], flipped[64:]], axis=1))
     left = jnp.concatenate(rows, axis=0)
     lags = jnp.dot(left, high[...], preferred_element_type=jnp.float32)
     lags = lags + jnp.dot(left, low[...], preferred_element_type=jnp.float32)
-    out[...] = lags.reshape(A_BLK, 1, 64, 128)
+    for i in range(0, A_BLK, 2):
+        out[i, 0] = lags[32 * i : 32 * i + 64, :128]
+        out[i + 1, 0] = lags[32 * i : 32 * i + 64, 128:]
 
 
 def lag_tables():
-    bins = np.arange(128)
-    phases = (bins[:, None] * bins[None, :] % 128) * (2.0 * math.pi / 128)
-    table = np.concatenate([np.cos(phases), -np.sin(phases)], axis=0) / math.sqrt(128 * 128)
+    bins = np.arange(TILES)[:, None]
+    lags = np.arange(128)[None, :]
+    phases = (bins * lags % 128) * (2.0 * math.pi / 128)
+    sines = -np.sin(phases)
+    sines[0] = np.cos(math.pi * np.arange(128))
+    table = np.zeros((2, 2, TILES, 2, 128))
+    for i in range(2):
+        table[0, i, :, i] = np.cos(phases)
+        table[1, i, :, i] = sines
+    table = table.reshape(4 * TILES, 256) / math.sqrt(128 * 128)
     high = table.astype(jnp.bfloat16)
     low = (table - high.astype(np.float64)).astype(jnp.bfloat16)
     return high, low
@@ -332,13 +378,16 @@
     vmem = pl.BlockSpec(memory_space=pltpu.VMEM)
     stack = pl.pallas_call(
         gather_stack,
-        out_shape=jax.ShapeDtypeStruct((128, 128, 128), jnp.float32),
-        in_specs=[vmem, vmem],
+        out_shape=jax.ShapeDtypeStruct((128 * TILES, 128), jnp.float32),
+        in_specs=[pl.BlockSpec(memory_space=pl.ANY)] * 2,
         out_specs=vmem,
         scratch_shapes=[
             pltpu.VMEM((16, 64, 16, 128), jnp.bfloat16),
             pltpu.VMEM((16, 2, 64, 16, 128), jnp.bfloat16),
             pltpu.VMEM((16, 64, 16, 128), jnp.bfloat16),
+            pltpu.VMEM((TILES, 128, 512), jnp.bfloat16),
+            pltpu.VMEM(spectra.shape, spectra.dtype),
+            pltpu.VMEM((1, 128), jnp.int32),
             pltpu.VMEM((1024, 128), jnp.float32),
             pltpu.VMEM((5, 4, 8, 128), jnp.float32),
             pltpu.VMEM((1, 128), jnp.float32),
@@ -347,7 +396,7 @@
             dma((2, 4, 2)), dma((2, 4, 2)), dma((2, 4, 2)), dma((2, 4, 2)),
             dma((4, 4, 2)), dma((4, 4, 2)),
             dma((4, 2)), dma((2,)),
-            dma((5, 4)), dma((5, 4)),
+            dma((5, 4)), dma((5, 4)), dma((2,)),
         ],
         compiler_params=pltpu.CompilerParams(
             collective_id=0, has_side_effects=True, vmem_limit_bytes=40 << 20

time: 103 us -> 84.9 us (0.82); the launches traced: 101 us -> 84.7 us
  Pallas kernels: 99.3 us -> 83.1 us
    pallas_call x1, Pallas kernels: 12.8 us -> 3.41 us  [body(): pl.pallas_call(lag_kernel, grid=(128 // A_BLK,), out_shape=jax.ShapeDtype...]
    pallas_call x1, Pallas kernels: 86.5 us -> 79.7 us  [body(): pl.pallas_call(gather_stack, out_shape=jax.ShapeDtypeStruct((128 * TILES,...]
where the time goes in v2:
time: 84.9 us; the launch traced here: 84.7 us
  Pallas kernels  83.1 us (98%)
  local copies, waits for them, and re-layouts  1.61 us (2%)
    pallas_call x1, Pallas kernels, body(): pl.pallas_call(gather_stack, out_shape=jax.ShapeDtypeStruct((128 * TILES,...  79.7 us
    pallas_call x1, Pallas kernels, body(): pl.pallas_call(lag_kernel, grid=(128 // A_BLK,), out_shape=jax.ShapeDtype...  3.41 us

profile of v2, /device:TPU:6, one launch (start us, length us, event | category | flops | bytes accessed | tf_op | source)
XLA Modules:
  0.0 84.7 jit_solution(2005821373864819385)
XLA Ops:
  0.0 0.0 copy-start
  0.0 0.9 %copy-done = bf16[4,2,128,128]{3,2,1,0:T(8,128)(2,1)S(1)} copy-done((bf16[4,2,128,128]{3,2,1,0:T(8,128)(2,1)S(1)}, bf16[4,2,128,128]{3,2,1,0:T(8,128)(2,1)}, u32[]{:S(2)}) %copy-start) | copy-done | bytes 262168
  1.0 0.0 copy-start.3
  1.0 0.7 copy-done.3
  1.6 0.0 copy-start.1
  1.6 0.0 copy-start.2
  1.6 79.7 %gather_stack.1.stack = f32[8192,128]{1,0:T(8,128)S(1)} custom-call(bf16[4,2,128,128]{3,2,1,0:T(8,128)(2,1)S(1)} %copy-done, s32[1,128]{1,0:T(1,128)S(1)} %bitcast.1), custom_call_target="tpu_custom_call" | custom-call | tf_op jit(solution)/shard_map/gather_stack/pallas_call | solution.py:379
  81.3 0.0 copy-done.1
  81.3 0.0 copy-done.2
  81.3 3.4 %lags.1 = f32[128,1,64,128]{3,2,1,0:T(8,128)} custom-call(f32[8192,128]{1,0:T(8,128)S(1)} %gather_stack.1.stack, bf16[256,256]{1,0:T(8,128)(2,1)S(1)} %copy-done.2, bf16[256,256]{1,0:T(8,128)(2,1)S(1)} %copy-done.1), custom_call_target="tpu_custom_call" | custom-call | tf_op jit(solution)/shard_map/lags/pallas_call | solution.py:407
Async XLA Ops:
  0.0 0.9 %copy-start = (bf16[4,2,128,128]{3,2,1,0:T(8,128)(2,1)S(1)}, bf16[4,2,128,128]{3,2,1,0:T(8,128)(2,1)}, u32[]{:S(2)}) copy-start(bf16[4,2,128,128]{3,2,1,0:T(8,128)(2,1)} %spectra_hbm.1) | copy-start | bytes 786436
  1.0 0.7 copy-start.3
  1.6 79.7 %copy-start.1 = (bf16[256,256]{1,0:T(8,128)(2,1)S(1)}, bf16[256,256]{1,0:T(8,128)(2,1)}, u32[]{:S(2)}) copy-start(bf16[256,256]{1,0:T(8,128)(2,1)} %constant.5.clone.low) | copy-start | bytes 393220
  1.6 79.7 %copy-start.2 = (bf16[256,256]{1,0:T(8,128)(2,1)S(1)}, bf16[256,256]{1,0:T(8,128)(2,1)}, u32[]{:S(2)}) copy-start(bf16[256,256]{1,0:T(8,128)(2,1)} %constant.4.clone.high) | copy-start | bytes 393220

commit v3 on v2

--- a/solution.py
+++ b/solution.py
@@ -14,8 +14,8 @@
 WAVES = 2
 CHUNK = 16
 WAVE = 2 * CHUNK
-REACH = ((8, 4), (4, 8))
-ORDER = [(1, 0)] + [(_w, _s) for _s in range(1, 9) for _w in range(WAVES)]
+BLOCK = 4
+ORDER = [(1, 0)] + [(_w, _s) for _s in range(1, 5) for _w in range(WAVES)]
 TILES = 64
 STEP = 8
 
@@ -89,15 +89,19 @@
             copy.wait()
         return jnp.sum(ebuf[k, : rounds[k][2]], axis=0)
 
+    def z_part(side, s, w, h):
+        slot = (z - s + 16) % 16 if side == 0 else (z + s) % 16
+        return zbuf.at[slot, pl.ds(w * WAVE + h * CHUNK, CHUNK)]
+
     def z_copy(side, s, w, h):
-        slot = (z - s + 16) % 16 if side == 0 else (z + s) % 16
-        part = zbuf.at[slot, pl.ds(w * WAVE + h * CHUNK, CHUNK)]
-        return remote(part, part, zs.at[side, s, w, h], zr.at[side, s, w, h], at(dz=1 if side == 0 else -1))
+        part = z_part(side, s, w, h)
+        hops = (1 if s < BLOCK else BLOCK) * (1 if side == 0 else -1)
+        return remote(part, part, zs.at[side, s, w, h], zr.at[side, s, w, h], at(dz=hops))
 
     def z_arrived(side, s, w, h):
-        slot = (z - s + 16) % 16 if side == 0 else (z + s) % 16
-        part = zbuf.at[slot, pl.ds(w * WAVE + h * CHUNK, CHUNK)]
-        remote(part, part, zs.at[side, s - 1, w, h], zr.at[side, s - 1, w, h], at(dz=1)).wait_recv()
+        part = z_part(side, s, w, h)
+        sent = min(s - 1, BLOCK)
+        remote(part, part, zs.at[side, sent, w, h], zr.at[side, sent, w, h], at(dz=1)).wait_recv()
 
     def wave(w):
         return pl.ds(w * WAVE, WAVE)
@@ -204,24 +208,17 @@
             pl.when(zl + s < 4)(lambda: act(zl + s))
 
     def z_step(w, s):
-        if s == 0:
-            for side in range(2):
-                for h in ((0, 1) if side == 0 else (1, 0)):
-                    z_copy(side, 0, w, h).start()
-        else:
-            for h in range(2):
-                for side in ((0, 1) if h == 0 else (1, 0)):
-                    if s <= REACH[h][side]:
-                        z_arrived(side, s, w, h)
-                        if s < REACH[h][side]:
-                            z_copy(side, s, w, h).start()
+        for h in range(2):
+            for side in (h, 1 - h):
+                if s > 0:
+                    z_arrived(side, s, w, h)
+                if s < BLOCK or side == h:
+                    z_copy(side, s, w, h).start()
         if s == 0:
             y_send(0, w)
-        if s == 4:
+        if s == BLOCK:
             y_send(1, w)
             y_send(2, w)
-        if s == 8:
-            y_send(3, w)
         in_block(s, lambda unit: x_send(unit, w))
         if s == 3:
             own_b(w).start()
@@ -231,27 +228,20 @@
             y_pass(0, w)
         if s == 4:
             y_end(0, w)
-        if s == 6:
-            y_pass(1, w)
-            y_pass(2, w)
-        if s == 8:
-            y_end(1, w)
-            y_end(2, w)
+
+    def z_last(w):
+        for side in range(2):
+            z_arrived(side, 2 * BLOCK, w, side)
+        y_send(3, w)
 
     energy_start(0, total)
     z_step(0, 0)
     stage = 0
     for w, s in ORDER:
         z_step(w, s)
-        if w == 0 and stage < 5:
-            value = energy_finish(stage)
+        if w == 0:
+            energy_start(stage + 1, energy_finish(stage))
             stage += 1
-            if stage < 5:
-                energy_start(stage, value)
-            else:
-                members = channels * lax.axis_size("row") * lax.axis_size("col")
-                energy = jnp.sum(value, axis=0, keepdims=True) / (members * 2 * 128) + EPSILON
-                factor[...] = kept[...].astype(jnp.float32) / energy
 
     def finish_b(w):
         for unit in range(4):
@@ -309,17 +299,29 @@
         return act
 
     for w in range(WAVES):
+        y_pass(1, w)
+        y_pass(2, w)
+        in_block(3, lambda unit: x_pass(unit, w))
+    value = energy_finish(4)
+    members = channels * lax.axis_size("row") * lax.axis_size("col")
+    energy = jnp.sum(value, axis=0, keepdims=True) / (members * 2 * 128) + EPSILON
+    factor[...] = kept[...].astype(jnp.float32) / energy
+    for w in range(WAVES):
         finish_b(w)
         over_tiles(w, make_rhs)
-        y_pass(3, w)
+        y_end(1, w)
+        y_end(2, w)
+        z_last(w)
+    y_pass(3, 0)
     for w in range(WAVES):
         finish_a(0, w)
-        over_tiles(w, make_stack([0]))
-    for w in range(WAVES):
-        y_end(3, w)
         finish_a(1, w)
         finish_a(2, w)
-        over_tiles(w, make_stack([1, 2]))
+        over_tiles(w, make_stack([0, 1, 2]))
+        if w == 0:
+            y_pass(3, 1)
+            y_end(3, 0)
+    y_end(3, 1)
     for w in range(WAVES):
         finish_a(3, w)
         over_tiles(w, make_stack([3]))
@@ -327,7 +329,7 @@
     for w in range(WAVES):
         for side in range(2):
             for h in range(2):
-                for s in range(REACH[h][side]):
+                for s in range(BLOCK + (side == h)):
                     z_copy(side, s, w, h).wait_send()
             for unit in range(4):
                 x_first(side, unit, w).wait_send()
@@ -379,7 +381,7 @@
     stack = pl.pallas_call(
         gather_stack,
         out_shape=jax.ShapeDtypeStruct((128 * TILES, 128), jnp.float32),
-        in_specs=[pl.BlockSpec(memory_space=pl.ANY)] * 2,
+        in_specs=[pl.BlockSpec(memory_space=pltpu.HBM)] * 2,
         out_specs=vmem,
         scratch_shapes=[
             pltpu.VMEM((16, 64, 16, 128), jnp.bfloat16),
@@ -391,7 +393,7 @@
             pltpu.VMEM((1024, 128), jnp.float32),
             pltpu.VMEM((5, 4, 8, 128), jnp.float32),
             pltpu.VMEM((1, 128), jnp.float32),
-            dma((2, 8, 2, 2)), dma((2, 8, 2, 2)),
+            dma((2, 5, 2, 2)), dma((2, 5, 2, 2)),
             dma((2, 4, 2)), dma((2, 4, 2)), dma((2, 4, 2)), dma((2, 4, 2)),
             dma((2, 4, 2)), dma((2, 4, 2)), dma((2, 4, 2)), dma((2, 4, 2)),
             dma((4, 4, 2)), dma((4, 4, 2)),

time: 84.9 us -> 81.5 us (0.960)
  Pallas kernels: 83.1 us -> 79.2 us
    pallas_call x1, Pallas kernels: 79.7 us -> 75.8 us  [body(): pl.pallas_call(gather_stack, out_shape=jax.ShapeDtypeStruct((128 * TILES,...]
where the time goes in v3:
time: 81.5 us; the launch traced here: 80.8 us
  Pallas kernels  79.2 us (97%)
  local copies, waits for them, and re-layouts  1.61 us (2%)
    pallas_call x1, Pallas kernels, body(): pl.pallas_call(gather_stack, out_shape=jax.ShapeDtypeStruct((128 * TILES,...  75.8 us
    pallas_call x1, Pallas kernels, body(): pl.pallas_call(lag_kernel, grid=(128 // A_BLK,), out_shape=jax.ShapeDtype...  3.41 us

profile of v3, /device:TPU:6, one launch (start us, length us, event | category | flops | bytes accessed | tf_op | source)
XLA Modules:
  0.0 80.8 jit_solution(3427404562140387715)
XLA Ops:
  0.0 0.0 copy-start
  0.0 0.9 %copy-done = bf16[4,2,128,128]{3,2,1,0:T(8,128)(2,1)S(1)} copy-done((bf16[4,2,128,128]{3,2,1,0:T(8,128)(2,1)S(1)}, bf16[4,2,128,128]{3,2,1,0:T(8,128)(2,1)}, u32[]{:S(2)}) %copy-start) | copy-done | bytes 262168
  1.0 0.0 copy-start.3
  1.0 0.7 copy-done.3
  1.6 0.0 copy-start.1
  1.6 0.0 copy-start.2
  1.6 75.8 %gather_stack.1.stack = f32[8192,128]{1,0:T(8,128)S(1)} custom-call(bf16[4,2,128,128]{3,2,1,0:T(8,128)(2,1)S(1)} %copy-done, s32[1,128]{1,0:T(1,128)S(1)} %bitcast.1), custom_call_target="tpu_custom_call" | custom-call | tf_op jit(solution)/shard_map/gather_stack/pallas_call | solution.py:381
  77.4 0.0 copy-done.1
  77.4 0.0 copy-done.2
  77.4 3.4 %lags.1 = f32[128,1,64,128]{3,2,1,0:T(8,128)} custom-call(f32[8192,128]{1,0:T(8,128)S(1)} %gather_stack.1.stack, bf16[256,256]{1,0:T(8,128)(2,1)S(1)} %copy-done.2, bf16[256,256]{1,0:T(8,128)(2,1)S(1)} %copy-done.1), custom_call_target="tpu_custom_call" | custom-call | tf_op jit(solution)/shard_map/lags/pallas_call | solution.py:409
Async XLA Ops:
  0.0 0.9 %copy-start = (bf16[4,2,128,128]{3,2,1,0:T(8,128)(2,1)S(1)}, bf16[4,2,128,128]{3,2,1,0:T(8,128)(2,1)}, u32[]{:S(2)}) copy-start(bf16[4,2,128,128]{3,2,1,0:T(8,128)(2,1)} %spectra_hbm.1) | copy-start | bytes 786436
  1.0 0.7 copy-start.3
  1.6 75.8 %copy-start.1 = (bf16[256,256]{1,0:T(8,128)(2,1)S(1)}, bf16[256,256]{1,0:T(8,128)(2,1)}, u32[]{:S(2)}) copy-start(bf16[256,256]{1,0:T(8,128)(2,1)} %constant.5.clone.low) | copy-start | bytes 393220
  1.6 75.8 %copy-start.2 = (bf16[256,256]{1,0:T(8,128)(2,1)S(1)}, bf16[256,256]{1,0:T(8,128)(2,1)}, u32[]{:S(2)}) copy-start(bf16[256,256]{1,0:T(8,128)(2,1)} %constant.4.clone.high) | copy-start | bytes 393220

commit v4 on v3

--- a/solution.py
+++ b/solution.py
@@ -17,7 +17,7 @@
 BLOCK = 4
 ORDER = [(1, 0)] + [(_w, _s) for _s in range(1, 5) for _w in range(WAVES)]
 TILES = 64
-STEP = 8
+STEP = 16
 
 
 def gather_stack(spectra_hbm, kept_hbm, stack, zbuf, abuf, bbuf, rhs, spectra, kept, tmp, ebuf, factor,
@@ -299,9 +299,10 @@
         return act
 
     for w in range(WAVES):
+        in_block(3, lambda unit: x_pass(unit, w))
+    for w in range(WAVES):
         y_pass(1, w)
         y_pass(2, w)
-        in_block(3, lambda unit: x_pass(unit, w))
     value = energy_finish(4)
     members = channels * lax.axis_size("row") * lax.axis_size("col")
     energy = jnp.sum(value, axis=0, keepdims=True) / (members * 2 * 128) + EPSILON
@@ -341,7 +342,7 @@
                 core_copy(which, unit, w).wait_send()
 
 
-A_BLK = 32
+A_BLK = 64
 
 
 def lag_kernel(stack, high, low, out):

time: 81.5 us -> 80.2 us (0.984)
  Pallas kernels: 79.2 us -> 78 us
where the time goes in v4:
time: 80.2 us; the launch traced here: 79.7 us
  Pallas kernels  78 us (97%)
  local copies, waits for them, and re-layouts  1.61 us (2%)
    pallas_call x1, Pallas kernels, body(): pl.pallas_call(gather_stack, out_shape=jax.ShapeDtypeStruct((128 * TILES,...  75.2 us
    pallas_call x1, Pallas kernels, body(): pl.pallas_call(lag_kernel, grid=(128 // A_BLK,), out_shape=jax.ShapeDtype...  2.86 us
    unnamed x8, local copies, waits for them, and re-layouts  1.61 us

profile of v4, /device:TPU:6, one launch (start us, length us, event | category | flops | bytes accessed | tf_op | source)
XLA Modules:
  0.0 79.7 jit_solution(2214681414627260169)
XLA Ops:
  0.0 0.0 copy-start
  0.0 0.9 %copy-done = bf16[4,2,128,128]{3,2,1,0:T(8,128)(2,1)S(1)} copy-done((bf16[4,2,128,128]{3,2,1,0:T(8,128)(2,1)S(1)}, bf16[4,2,128,128]{3,2,1,0:T(8,128)(2,1)}, u32[]{:S(2)}) %copy-start) | copy-done | bytes 262168
  1.0 0.0 copy-start.3
  1.0 0.7 copy-done.3
  1.6 0.0 copy-start.1
  1.6 0.0 copy-start.2
  1.6 75.2 %gather_stack.1.stack = f32[8192,128]{1,0:T(8,128)S(1)} custom-call(bf16[4,2,128,128]{3,2,1,0:T(8,128)(2,1)S(1)} %copy-done, s32[1,128]{1,0:T(1,128)S(1)} %bitcast.1), custom_call_target="tpu_custom_call" | custom-call | tf_op jit(solution)/shard_map/gather_stack/pallas_call | solution.py:382
  76.8 0.0 copy-done.1
  76.8 0.0 copy-done.2
  76.8 2.9 %lags.1 = f32[128,1,64,128]{3,2,1,0:T(8,128)} custom-call(f32[8192,128]{1,0:T(8,128)S(1)} %gather_stack.1.stack, bf16[256,256]{1,0:T(8,128)(2,1)S(1)} %copy-done.2, bf16[256,256]{1,0:T(8,128)(2,1)S(1)} %copy-done.1), custom_call_target="tpu_custom_call" | custom-call | tf_op jit(solution)/shard_map/lags/pallas_call | solution.py:410
Async XLA Ops:
  0.0 0.9 %copy-start = (bf16[4,2,128,128]{3,2,1,0:T(8,128)(2,1)S(1)}, bf16[4,2,128,128]{3,2,1,0:T(8,128)(2,1)}, u32[]{:S(2)}) copy-start(bf16[4,2,128,128]{3,2,1,0:T(8,128)(2,1)} %spectra_hbm.1) | copy-start | bytes 786436
  1.0 0.7 copy-start.3
  1.6 75.2 %copy-start.1 = (bf16[256,256]{1,0:T(8,128)(2,1)S(1)}, bf16[256,256]{1,0:T(8,128)(2,1)}, u32[]{:S(2)}) copy-start(bf16[256,256]{1,0:T(8,128)(2,1)} %constant.5.clone.low) | copy-start | bytes 393220
  1.6 75.2 %copy-start.2 = (bf16[256,256]{1,0:T(8,128)(2,1)S(1)}, bf16[256,256]{1,0:T(8,128)(2,1)}, u32[]{:S(2)}) copy-start(bf16[256,256]{1,0:T(8,128)(2,1)} %constant.4.clone.high) | copy-start | bytes 393220
